TPU v7x, 32 devices: a whole 2x2x4 slice. The times are simulated.
32 devices in a mesh: groups: 2 (over y), dp: 4 (over x, core), tensor: 4 (over z).
Axes of the slice: x: 2, y: 2, z: 4, core: 2. Of those that a mesh axis runs over, the one named last changes fastest.
Arguments:
- hidden: bfloat16 [512, 8192], P(('groups', 'dp', 'tensor')), parts along dimension 0, may hold values from -6 to 6
- query_weight: bfloat16 [8192, 4096], P(None, 'tensor'), may hold values from -0.0625 to 0.0625
- adapter_shrink: bfloat16 [64, 8192, 64], P('dp', 'tensor'), may hold values from -0.0625 to 0.0625
- adapter_expand: bfloat16 [64, 64, 4096], P('dp', None, 'tensor'), may hold values from -0.75 to 0.75
- adapter_page_table: int32 [128], P('groups'), parts along dimension 0, may hold values from 0 to 63, as said below
- request_adapter_index: int32 [512], P(('groups', 'dp', 'tensor')), parts along dimension 0, may hold values from 0 to 63, as said below
- key_value_cache: bfloat16 [512, 128, 2, 512], P(('groups', 'dp', 'tensor')), parts along dimension 0, may hold values from -800 to 800
- cached_lengths: int32 [512], P(('groups', 'dp', 'tensor')), parts along dimension 0, may hold values from 16 to 128, as said below
Outputs:
- attended: bfloat16 [512, 4096], P(('groups', 'dp', 'tensor')), parts along dimension 0
There are 2 independent parts, one for each index of `groups`. A program takes and returns all parts, laid end to end along the dimension named above; an argument that names none is the same for every part. Nothing has to cross between parts.
Inputs may be any that keep to these rules, and one draw needn't show every extreme that they name: `adapter_page_table`: each replica's table is a permutation of the 64 pages; page p lies on dp index p // 16. `request_adapter_index`: among the 64 requests of one dp index, at most 24 use adapters whose pages lie on one dp index; in every replica one dp index's pages serve exactly 24 requests of every dp index. `cached_lengths`: some request of every replica has exactly 128 cached positions.
All inputs are finite; a program needn't handle non-finite values.
Results may differ from a plain program's by a relative error of at most 0.012.
The roundings to bfloat16 on the way count: a program that leaves them out, or rounds other values in their place, can miss the bound.
Values may be sent and summed in bfloat16 or wider, within the bound.
A program may use at most 128 MiB of HBM per device.

v0:
```python
import math

import jax
import jax.numpy as jnp
from jax import lax
from jax.sharding import PartitionSpec as P

QUERY_HEADS = 32
KVH = 4
HEAD_SIZE = 128


def page_lookup(adapter_page_table, adapters):
    matches = adapters[:, None] == jnp.arange(adapter_page_table.shape[0], dtype=jnp.int32)[None, :]
    return jnp.sum(jnp.where(matches, adapter_page_table[None, :], 0), axis=1)


def shrinking_rows(input_features, resident_pages, adapter_shrink):
    selected_pages = (
        resident_pages[:, None] == jnp.arange(adapter_shrink.shape[0], dtype=jnp.int32)[None, :]
    )
    combined_partials = jnp.einsum(
        "xw,owh->xoh", input_features, adapter_shrink, preferred_element_type=jnp.float32
    )
    return (
        jnp.sum(jnp.where(selected_pages[:, :, None], combined_partials, 0.0), axis=1),
        selected_pages,
    )


def expanded_rows(reduced_features, selected_pages, adapter_expand):
    spread_output = jnp.where(
        selected_pages[:, :, None], reduced_features[:, None, :], jnp.zeros((), jnp.bfloat16)
    )
    return jnp.einsum(
        "dbm,bmn->dn", spread_output, adapter_expand, preferred_element_type=jnp.float32
    )


def attend(queries, key_value_cache, cached_lengths):
    req_count = queries.shape[0]
    cache_len = key_value_cache.shape[1]
    queries = queries.reshape(req_count, KVH, QUERY_HEADS // KVH, HEAD_SIZE)
    key_rows = key_value_cache[:, :, 0, :].reshape(req_count, cache_len, KVH, HEAD_SIZE)
    values = key_value_cache[:, :, 1, :].reshape(req_count, cache_len, KVH, HEAD_SIZE)
    scores = jnp.einsum(
        "tkgd,tckd->tkgc", queries, key_rows, preferred_element_type=jnp.float32
    ) * (1.0 / math.sqrt(HEAD_SIZE))
    in_range = jnp.arange(cache_len, dtype=jnp.int32)[None, :] < cached_lengths[:, None]
    scores = jnp.where(in_range[:, None, None, :], scores, -jnp.inf)
    largest = jnp.max(scores, axis=-1, keepdims=True)
    powers = jnp.exp(scores - largest)
    weights = (powers / jnp.sum(powers, axis=-1, keepdims=True)).astype(jnp.bfloat16)
    mixture = jnp.einsum("tkgc,tckd->tkgd", weights, values, preferred_element_type=jnp.float32)
    return mixture.astype(jnp.bfloat16).reshape(req_count, QUERY_HEADS * HEAD_SIZE)


def local(
    hidden,
    query_weight,
    adapter_shrink,
    adapter_expand,
    adapter_page_table,
    request_adapter_index,
    key_value_cache,
    cached_lengths,
):
    own_count = hidden.shape[0]
    row_x, row_ids = (
        lax.all_gather(hidden, "tensor", axis=0, tiled=True),
        lax.all_gather(request_adapter_index, "tensor", axis=0, tiled=True),
    )
    row_count = row_x.shape[0]
    pages_row = page_lookup(adapter_page_table, row_ids)
    base_q = jnp.dot(row_x, query_weight, preferred_element_type=jnp.float32)
    block_span_width = adapter_shrink.shape[1]
    x_block = lax.dynamic_slice_in_dim(
        row_x, lax.axis_index("tensor") * block_span_width, block_span_width, 1
    )
    pages_per_holder = adapter_shrink.shape[0]
    owner_index = lax.axis_index("dp")
    dp_count = lax.axis_size("dp")
    slot_cap = 3 * row_count // (2 * dp_count)
    owner_of = pages_row // pages_per_holder
    owner_hits = (owner_of[:, None] == jnp.arange(dp_count, dtype=jnp.int32)[None, :]).astype(
        jnp.int32
    )
    before = jnp.cumsum(owner_hits, axis=0) - owner_hits
    position = jnp.sum(before * owner_hits, axis=1)
    slot_of = owner_of * slot_cap + position
    slot_token = (
        jnp.full((dp_count * slot_cap,), row_count, jnp.int32)
        .at[slot_of]
        .set(jnp.arange(row_count, dtype=jnp.int32))
    )
    padded_x = jnp.concatenate([x_block, jnp.zeros((1, block_span_width), jnp.bfloat16)], axis=0)
    padded_pages = jnp.concatenate([pages_row, jnp.full((1,), -1, jnp.int32)], axis=0)
    send_x = padded_x[slot_token].reshape(dp_count, slot_cap, block_span_width)
    send_pages = padded_pages[slot_token].reshape(dp_count, slot_cap)
    recv_x, recv_pages = (
        lax.all_to_all(send_x, "dp", split_axis=0, concat_axis=0, tiled=True),
        lax.all_to_all(send_pages, "dp", split_axis=0, concat_axis=0, tiled=True),
    )
    resident_pages = recv_pages.reshape(dp_count * slot_cap) - owner_index * pages_per_holder
    partial_total_sum, selected_pages = shrinking_rows(
        recv_x.reshape(dp_count * slot_cap, block_span_width), resident_pages, adapter_shrink
    )
    reduced_features = lax.psum(partial_total_sum, "tensor").astype(jnp.bfloat16)
    slot_delta = expanded_rows(reduced_features, selected_pages, adapter_expand).reshape(
        dp_count, slot_cap, -1
    )
    returned = lax.all_to_all(slot_delta, "dp", split_axis=0, concat_axis=0, tiled=True)
    correction = returned.reshape(dp_count * slot_cap, -1)[slot_of]
    query_rows = (base_q + correction).astype(jnp.bfloat16)
    tensor_count = lax.axis_size("tensor")
    query_send = query_rows.reshape(tensor_count, own_count, query_rows.shape[1])
    query_own = lax.all_to_all(query_send, "tensor", split_axis=0, concat_axis=2, tiled=True)
    return attend(
        query_own.reshape(own_count, QUERY_HEADS * HEAD_SIZE), key_value_cache, cached_lengths
    )


def solution(mesh):
    in_specs = (
        P(("groups", "dp", "tensor"), None),
        P(None, "tensor"),
        P("dp", "tensor", None),
        P("dp", None, "tensor"),
        P("groups"),
        P(("groups", "dp", "tensor")),
        P(("groups", "dp", "tensor"), None, None, None),
        P(("groups", "dp", "tensor")),
    )
    out_specs = P(("groups", "dp", "tensor"), None)
    return jax.shard_map(local, mesh=mesh, in_specs=in_specs, out_specs=out_specs, check_vma=False)
```

profile of v0, /device:TPU:0, one launch (start us, length us, event | category | flops | bytes accessed | tf_op | source)
XLA Modules:
  0.0 143.5 jit_solution(8206091274765026861)
XLA Ops:
  6.5 0.0 copy-start
  6.5 0.0 all-gather.2.cloned.1.call-start
  6.5 0.7 all-gather.2.cloned.1.call-update
  7.3 1.2 dynamic-slice
  9.2 0.9 dynamic-update-slice
  10.0 9.9 %all-reduce.1 = s32[64]{0:T(128)S(1)} all-reduce(s32[64]{0:T(128)S(1)} %dynamic-update-slice), channel_id=1, replica_groups=mesh['groups'=2,'dp'=4,'tensor'=4] {'tensor'}, use_global_device_ids=true, to_apply=%add.1 | all-reduce | flops 64 | bytes 512
  19.9 0.8 select_reduce_fusion.2
  20.8 0.1 fusion.12
  20.8 0.1 reduce_window_sum.11
  20.9 0.2 select_reduce_fusion.1
  21.2 0.8 scatter_custom_fusion
  21.9 0.1 pad_add_fusion
  22.0 1.2 gather_fusion
  23.3 0.7 all_to_all.23
  23.9 3.2 %all-to-all-start = ((s32[4,1,24]{2,1,0:T(1,128)}), s32[4,1,24]{2,1,0:T(1,128)S(1)}, u32[]{:S(2)}, u32[]{:S(2)}) async-start(s32[4,1,24]{2,1,0:T(1,128)} %bitcast.4), calls=%async_computation | async-start | bytes 4096 | tf_op jit(solution)/shard_map/all_to_all | solution.py:102
  27.2 12.5 %all-gather.2.cloned.1.call-done = bf16[64,8192]{1,0:T(8,128)(2,1)} async-done(((bf16[16,8192]{1,0:T(8,128)(2,1)}), bf16[64,8192]{1,0:T(8,128)(2,1)}) %all-gather.2.cloned.1.call-update) | async-done | bytes 1048592 | tf_op jit(solution)/shard_map/all_gather | solution.py:70
  39.7 1.0 constant_dynamic-slice_fusion
  40.7 1.6 %gather_fusion.1 = bf16[96,2048]{1,0:T(8,128)(2,1)} fusion(bf16[65,2048]{1,0:T(8,128)(2,1)S(1)} %concatenate.7, s32[1024]{0:T(1024)S(1)} %pad_clamp_fusion.1), kind=kCustom, calls=%fused_computation.1 | custom fusion | bytes 786816 | tf_op jit(solution)/shard_map/gather | solution.py:98
  42.3 0.0 all-to-all-done
  42.3 3.5 %all-to-all-start.1 = ((bf16[4,24,2048]{2,1,0:T(8,128)(2,1)}), bf16[4,24,2048]{2,1,0:T(8,128)(2,1)S(1)}, u32[]{:S(2)}, u32[]{:S(2)}) async-start(bf16[4,24,2048]{2,1,0:T(8,128)(2,1)} %bitcast.5), calls=%async_computation.1 | async-start | bytes 786432 | tf_op jit(solution)/shard_map/all_to_all | solution.py:101
  45.8 0.1 sub.37
  45.9 7.3 %all-to-all-done.1 = bf16[4,24,2048]{2,1,0:T(8,128)(2,1)S(1)} async-done(((bf16[4,24,2048]{2,1,0:T(8,128)(2,1)}), bf16[4,24,2048]{2,1,0:T(8,128)(2,1)S(1)}, u32[]{:S(2)}, u32[]{:S(2)}) %all-to-all-start.1) | async-done | bytes 393248 | tf_op jit(solution)/shard_map/all_to_all | solution.py:101
  53.1 3.4 %fusion.19 = f32[96,1024]{0,1:S(1)} fusion(bf16[96,2048]{1,0:T(8,128)(2,1)S(1)} %bitcast.60, bf16[2048,1024]{0,1:T(8,128)(2,1)} %bitcast.57), kind=kOutput, calls=%fused_computation.52 | convolution fusion | flops 402653184 | bytes 4980736
  56.6 0.1 select_reduce_fusion
  56.7 17.5 %psum.7 = bf16[96,64]{0,1:T(8,128)(2,1)S(1)} all-reduce(f32[96,64]{0,1:T(8,128)S(1)} %select_reduce_fusion), channel_id=1, replica_groups=mesh['groups'=2,'dp'=4,'tensor'=4] {'tensor'}, use_global_device_ids=true, to_apply=%region_5.6 | all-reduce | flops 6144 | bytes 36864 | tf_op jit(solution)/shard_map/psum | solution.py:108
  74.2 0.0 copy-done
  74.2 1.3 fusion.5
  75.4 3.5 %all-to-all-start.2 = ((f32[4,24,1024]{2,1,0:T(8,128)}), f32[4,24,1024]{2,1,0:T(8,128)S(1)}, u32[]{:S(2)}, u32[]{:S(2)}) async-start(f32[4,24,1024]{2,1,0:T(8,128)} %bitcast.11), calls=%async_computation.2 | async-start | bytes 786432 | tf_op jit(solution)/shard_map/all_to_all | solution.py:112
  78.9 9.9 %fusion.17 = (bf16[16,128,1,512]{3,2,1,0:T(2,128)(2,1)}, bf16[16,128,1,512]{3,2,1,0:T(2,128)(2,1)}) fusion(bf16[16,128,2,512]{3,2,1,0:T(2,128)(2,1)} %param.14), kind=kLoop, calls=%fused_computation.50 | loop fusion | bytes 8388608 | tf_op jit(solution)/shard_map/slice | solution.py:44
  88.8 10.5 %copy.31 = bf16[16,128,1,512]{1,3,0,2:T(8,128)(2,1)} copy(bf16[16,128,1,512]{3,2,1,0:T(2,128)(2,1)} %get-tuple-element.6) | data formatting | bytes 4194304
  99.4 0.0 copy-start.1
  99.4 10.6 %copy.30 = bf16[16,128,1,512]{1,3,0,2:T(8,128)(2,1)} copy(bf16[16,128,1,512]{3,2,1,0:T(2,128)(2,1)} %get-tuple-element.5) | data formatting | bytes 4194304
  110.0 0.0 all-to-all-done.2
  110.0 1.4 gather_fusion.2
  111.4 0.0 copy-done.1
  111.4 0.0 copy-start.2
  111.4 9.5 %fusion.4 = bf16[64,1024]{1,0:T(8,128)(2,1)} fusion(f32[64,1024]{1,0:T(8,128)} %gather_fusion.2, bf16[64,8192]{1,0:T(8,128)(2,1)S(1)} %copy-done.1, bf16[8192,1024]{1,0:T(8,128)(2,1)} %param.9), kind=kOutput, calls=%fused_computation.11 | convolution fusion | flops 1073872896 | bytes 18219008 | tf_op jit(solution)/shard_map/dot_general | solution.py:75
  120.8 3.3 %all-to-all-start.3 = ((bf16[4,16,1024]{2,1,0:T(8,128)(2,1)}), bf16[4,16,1024]{2,1,0:T(8,128)(2,1)S(1)}, u32[]{:S(2)}, u32[]{:S(2)}) async-start(bf16[4,16,1024]{2,1,0:T(8,128)(2,1)} %bitcast.13), calls=%async_computation.3 | async-start | bytes 262144 | tf_op jit(solution)/shard_map/all_to_all | solution.py:117
  124.2 0.0 copy-done.2
  124.2 0.1 iota_compare_fusion.3
  124.2 6.4 %all-to-all-done.3 = bf16[4,16,1024]{2,1,0:T(8,128)(2,1)S(1)} async-done(((bf16[4,16,1024]{2,1,0:T(8,128)(2,1)}), bf16[4,16,1024]{2,1,0:T(8,128)(2,1)S(1)}, u32[]{:S(2)}, u32[]{:S(2)}) %all-to-all-start.3) | async-done | bytes 131104 | tf_op jit(solution)/shard_map/all_to_all | solution.py:117
  130.6 2.2 %fusion.2 = f32[16,4,8,128]{3,2,1,0:T(8,128)S(1)} fusion(bf16[16,128,4,128]{1,3,2,0:T(8,128)(2,1)} %bitcast.56, bf16[16,4,8,128]{3,2,0,1:T(8,128)(2,1)S(1)} %bitcast.61, pred[16,128]{1,0:T(8,128)(4,1)S(1)} %iota_compare_fusion.3), kind=kOutput, calls=%fused_computation.8 | convolution fusion | flops 16908288 | bytes 2492416 | tf_op jit(solution)/shard_map/tkgd,tckd->tkgc/dot_general | solution.py:46
  132.9 0.3 fusion.18
  133.1 2.8 %convolution_convert_fusion = bf16[16,4,8,128]{3,2,1,0:T(8,128)(2,1)S(1)} fusion(bf16[16,128,4,128]{1,3,2,0:T(8,128)(2,1)} %bitcast.58, f32[16,4,8]{2,1,0:T(4,128)S(1)} %fusion.18, f32[16,4,8,128]{3,2,1,0:T(8,128)S(1)} %fusion.2), kind=kOutput, calls=%fused_computation.10 | convolution fusion | flops 17040000 | bytes 2492416 | tf_op jit(solution)/shard_map/tkgc,tckd->tkgd/dot_general | solution.py:54
  136.0 0.7 copy.37
  (11 shorter events, 0.1 us)
Async XLA Ops:
  6.5 67.6 %copy-start = (bf16[16,64,1024]{2,1,0:T(8,128)(2,1)S(1)}, bf16[16,64,1024]{2,1,0:T(8,128)(2,1)}, u32[]{:S(2)}) copy-start(bf16[16,64,1024]{2,1,0:T(8,128)(2,1)} %param.11) | copy-start | bytes 6291460
  6.5 33.2 %all-gather.2.cloned.1.call-start = ((), (), s32[]{:S(2)}) async-start(), calls=%async_computation.4 | async-start | bytes 1310720 | tf_op jit(solution)/shard_map/all_gather | solution.py:70
  23.9 18.3 %all-to-all-start = ((s32[4,1,24]{2,1,0:T(1,128)}), s32[4,1,24]{2,1,0:T(1,128)S(1)}, u32[]{:S(2)}, u32[]{:S(2)}) async-start(s32[4,1,24]{2,1,0:T(1,128)} %bitcast.4), calls=%async_computation | async-start | bytes 4096 | tf_op jit(solution)/shard_map/all_to_all | solution.py:102
  42.3 10.9 %all-to-all-start.1 = ((bf16[4,24,2048]{2,1,0:T(8,128)(2,1)}), bf16[4,24,2048]{2,1,0:T(8,128)(2,1)S(1)}, u32[]{:S(2)}, u32[]{:S(2)}) async-start(bf16[4,24,2048]{2,1,0:T(8,128)(2,1)} %bitcast.5), calls=%async_computation.1 | async-start | bytes 786432 | tf_op jit(solution)/shard_map/all_to_all | solution.py:101
  75.4 34.5 %all-to-all-start.2 = ((f32[4,24,1024]{2,1,0:T(8,128)}), f32[4,24,1024]{2,1,0:T(8,128)S(1)}, u32[]{:S(2)}, u32[]{:S(2)}) async-start(f32[4,24,1024]{2,1,0:T(8,128)} %bitcast.11), calls=%async_computation.2 | async-start | bytes 786432 | tf_op jit(solution)/shard_map/all_to_all | solution.py:112
  99.4 12.0 %copy-start.1 = (bf16[64,8192]{1,0:T(8,128)(2,1)S(1)}, bf16[64,8192]{1,0:T(8,128)(2,1)}, u32[]{:S(2)}) copy-start(bf16[64,8192]{1,0:T(8,128)(2,1)} %all-gather.2.cloned.1.call-done) | copy-start | bytes 3145732
  111.4 12.8 %copy-start.2 = (s32[16]{0:T(128)S(1)}, s32[16]{0:T(128)}, u32[]{:S(2)}) copy-start(s32[16]{0:T(128)} %param.15) | copy-start | bytes 196
  120.8 9.8 %all-to-all-start.3 = ((bf16[4,16,1024]{2,1,0:T(8,128)(2,1)}), bf16[4,16,1024]{2,1,0:T(8,128)(2,1)S(1)}, u32[]{:S(2)}, u32[]{:S(2)}) async-start(bf16[4,16,1024]{2,1,0:T(8,128)(2,1)} %bitcast.13), calls=%async_computation.3 | async-start | bytes 262144 | tf_op jit(solution)/shard_map/all_to_all | solution.py:117
Sparse Core Ops, SparseCore 0:
  8.9 30.7 all-gather.1
where the time goes:
time: 145 us; the launch traced here: 144 us
  local copies, waits for them, and re-layouts  40.6 us (28%)
  blocking collectives  27.4 us (19%)
  waiting for transfers between devices  26.9 us (19%)
  matrix products  19.2 us (13%)
  between operations  14.2 us (10%)
  starting transfers between devices  13.5 us (9%)
  other arithmetic  1.74 us (1%)
    unnamed x13, local copies, waits for them, and re-layouts  24 us
    psum x1, blocking collectives, local(): lax.psum(partial_total_sum, 'tensor').astype(jnp.bfloat16)  17.5 us
    all_gather x1, waiting for transfers between devices, local(): lax.all_gather(hidden, 'tensor', axis=0, tiled=True)  12.5 us
    slice x1, local copies, waits for them, and re-layouts, attend(): key_value_cache[:, :, 0, :].reshape(req_count, cache_len, KVH, HEAD_SIZE)  9.93 us
    unnamed x1, blocking collectives  9.89 us
    dot_general x1, matrix products, local(): base_q = jnp.dot(row_x, query_weight, preferred_element_type=jnp.float32)  9.46 us
    all_to_all x1, waiting for transfers between devices, local(): lax.all_to_all(send_x, 'dp', split_axis=0, concat_axis=0, tiled=True)  7.29 us
    all_to_all x1, waiting for transfers between devices, local(): lax.all_to_all(query_send, 'tensor', split_axis=0, concat_axis=2, tiled=T...  6.38 us
  transfers between devices with their start and end apart: 5, of which 3 were waited for; matrix products, arithmetic and copies ran while one was open for 27% of the time, Pallas kernels for 0%

commit v1 on v0

v1 whole, which is shorter than its diff:
```python
import functools
import math

import jax
import jax.numpy as jnp
from jax import lax
from jax.experimental import pallas as pl
from jax.experimental.pallas import tpu as pltpu
from jax.sharding import PartitionSpec as P

QUERY_HEADS = 32
KVH = 4
HEAD_SIZE = 128
MESH = pl.DeviceIdType.MESH
F32 = jnp.float32
BF16 = jnp.bfloat16


def dot(a, b, dims=((1,), (0,)), precision=None):
    return lax.dot_general(a, b, (dims, ((), ())), preferred_element_type=F32, precision=precision)


def query_kernel(
    hidden, pages, weight, shrink, expand,
    out,
    xg, pg, wv, sv, ev, xsend, xrecv, part, parts, ret_send, ret_recv, qsend, base,
    w_sem, s_sem, e_sem, own_sem, pg_send, pg_recv, x_send, x_recv,
    d_send, d_recv, p_send, p_recv, r_send, r_recv, q_send, q_recv,
):
    nt, nd = lax.axis_size("tensor"), lax.axis_size("dp")
    t, g = lax.axis_index("tensor"), lax.axis_index("dp")
    own, width = hidden.shape
    rows = own * nt
    span = width // nt
    holders, rank = shrink.shape[0], shrink.shape[2]
    cols = weight.shape[1]
    slots = xsend.shape[0] // nd
    cap = 3 * rows // (2 * nd)
    cap = -(-cap // 8) * 8

    def tpeer(d):
        return lax.rem(t + d, nt)

    def dpeer(d):
        return lax.rem(g + d, nd)

    def mult(x, m):
        return pl.multiple_of(x * m, m)

    def w_copy(c):
        block = lax.rem(t + c, nt)
        return pltpu.make_async_copy(weight.at[pl.ds(mult(block, span), span), :], wv.at[c], w_sem.at[c])

    s_copy = pltpu.make_async_copy(shrink, sv, s_sem)
    e_copy = pltpu.make_async_copy(expand, ev, e_sem)
    w_copy(0).start()
    s_copy.start()
    for c in range(1, nt):
        w_copy(c).start()
    e_copy.start()

    ret_recv[...] = jnp.zeros_like(ret_recv)
    barrier = pltpu.get_barrier_semaphore()

    @pl.loop(1, nt)
    def _(d):
        pl.semaphore_signal(barrier, inc=1, device_id={"tensor": tpeer(d)}, device_id_type=MESH)

    @pl.loop(1, nd)
    def _(d):
        pl.semaphore_signal(barrier, inc=1, device_id={"dp": dpeer(d)}, device_id_type=MESH)

    pl.semaphore_wait(barrier, nt + nd - 2)

    my_rows = pl.ds(mult(t, own), own)

    def pg_copy(d):
        return pltpu.make_async_remote_copy(
            src_ref=pages, dst_ref=pg.at[my_rows, :], send_sem=pg_send.at[d], recv_sem=pg_recv.at[d],
            device_id={"tensor": tpeer(d)}, device_id_type=MESH)

    def x_copy(c, d):
        block = lax.rem(t + d + c, nt)
        return pltpu.make_async_remote_copy(
            src_ref=hidden.at[:, pl.ds(mult(block, span), span)], dst_ref=xg.at[c, my_rows, :],
            send_sem=x_send.at[c, d], recv_sem=x_recv.at[c, d],
            device_id={"tensor": tpeer(d)}, device_id_type=MESH)

    @pl.loop(1, nt)
    def _(d):
        pg_copy(d).start()
        x_copy(0, d).start()

    @pl.loop(1, nt)
    def _(c):
        @pl.loop(1, nt)
        def _(d):
            x_copy(c, d).start()

    def own_copy(c):
        block = lax.rem(t + c, nt)
        return pltpu.make_async_copy(
            hidden.at[:, pl.ds(mult(block, span), span)], xg.at[c, my_rows, :], own_sem.at[c])

    @pl.loop(0, nt)
    def _(c):
        own_copy(c).start()

    pg[my_rows, :] = pages[...]

    def wait_block(c):
        own_copy(c).wait()

        @pl.loop(1, nt)
        def _(d):
            x_copy(c, d).wait_recv()

    @pl.loop(1, nt)
    def _(d):
        pg_copy(d).wait_recv()

    page_all = pg[...]
    page_col = page_all[:, 0:1]
    lane = lax.broadcasted_iota(jnp.int32, (rows, 128), 1)
    hits = ((page_all >= lane * holders) & (page_all < (lane + 1) * holders)).astype(F32)
    lower = (lax.broadcasted_iota(jnp.int32, (rows, rows), 1)
             < lax.broadcasted_iota(jnp.int32, (rows, rows), 0)).astype(F32)
    before = dot(lower.astype(BF16), hits.astype(BF16))
    slot_of = jnp.sum(hits * (before + lane.astype(F32) * slots), axis=1, keepdims=True).astype(jnp.int32)
    place = (slot_of == lax.broadcasted_iota(jnp.int32, (rows, nd * slots), 1)).astype(F32).astype(BF16)
    page_bf = (page_all + 1).astype(F32).astype(BF16)

    wait_block(0)
    xsend[:, :span] = dot(place, xg[0], ((0,), (0,))).astype(BF16)
    xsend[:, span:] = dot(place, page_bf, ((0,), (0,))).astype(BF16)

    my_slots = pl.ds(mult(g, slots), slots)

    def d_copy(d):
        p = dpeer(d)
        return pltpu.make_async_remote_copy(
            src_ref=xsend.at[pl.ds(mult(p, slots), slots), :], dst_ref=xrecv.at[my_slots, :],
            send_sem=d_send.at[d], recv_sem=d_recv.at[d], device_id={"dp": p}, device_id_type=MESH)

    @pl.loop(1, nd)
    def _(d):
        d_copy(d).start()

    xrecv[my_slots, :] = xsend[my_slots, :]

    w_copy(0).wait()
    tile = min(cols, 256)

    def base_add(c, first):
        @pl.loop(0, cols // tile)
        def _(j):
            at = pl.ds(mult(j, tile), tile)
            term = dot(xg[c], wv[c, :, at])
            base[:, at] = term if first else base[:, at] + term

    base_add(0, True)
    s_copy.wait()

    @pl.loop(1, nd)
    def _(d):
        d_copy(d).wait_recv()

    resident = (xrecv[:, span:span + 128].astype(F32)).astype(jnp.int32)[:, 0:1] - 1 - g * holders
    part[...] = jnp.zeros_like(part)

    @pl.loop(0, holders)
    def _(o):
        y = dot(xrecv[:, :span], sv[o])
        part[:, :rank] = part[:, :rank] + jnp.where(resident == o, y, 0.0)

    def p_copy(d):
        return pltpu.make_async_remote_copy(
            src_ref=part, dst_ref=parts.at[t], send_sem=p_send.at[d], recv_sem=p_recv.at[d],
            device_id={"tensor": tpeer(d)}, device_id_type=MESH)

    @pl.loop(1, nt)
    def _(d):
        p_copy(d).start()

    parts[t] = part[...]

    @pl.loop(1, nt)
    def _(c):
        wait_block(c)
        w_copy(c).wait()
        base_add(c, False)

    e_copy.wait()

    @pl.loop(1, nt)
    def _(d):
        p_copy(d).wait_recv()

    total = parts[0]
    for i in range(1, nt):
        total = total + parts[i]
    reduced = total[:, :rank].astype(BF16).astype(F32)
    spread = jnp.concatenate(
        [jnp.where(resident == o, reduced, 0.0) for o in range(holders)], axis=1).astype(BF16)
    ret_send[...] = dot(spread, ev[...])

    def r_copy(d):
        p = dpeer(d)
        return pltpu.make_async_remote_copy(
            src_ref=ret_send.at[pl.ds(mult(p, slots), cap), :],
            dst_ref=ret_recv.at[pl.ds(mult(g, slots), cap), :],
            send_sem=r_send.at[d], recv_sem=r_recv.at[d], device_id={"dp": p}, device_id_type=MESH)

    @pl.loop(1, nd)
    def _(d):
        r_copy(d).start()

    ret_recv[my_slots, :] = ret_send[my_slots, :]

    @pl.loop(1, nd)
    def _(d):
        r_copy(d).wait_recv()

    high = ret_recv[...].astype(BF16)
    low = (ret_recv[...] - high.astype(F32)).astype(BF16)
    qsend[...] = (base[...] + (dot(place, high) + dot(place, low))).astype(BF16)

    def q_copy(d):
        p = tpeer(d)
        return pltpu.make_async_remote_copy(
            src_ref=qsend.at[pl.ds(mult(p, own), own), :], dst_ref=out.at[t],
            send_sem=q_send.at[d], recv_sem=q_recv.at[d],
            device_id={"tensor": p}, device_id_type=MESH)

    @pl.loop(1, nt)
    def _(d):
        q_copy(d).start()

    out[t] = qsend[my_rows, :]

    @pl.loop(1, nt)
    def _(d):
        q_copy(d).wait_recv()

    @pl.loop(1, nt)
    def _(d):
        pg_copy(d).wait_send()
        p_copy(d).wait_send()
        q_copy(d).wait_send()

        @pl.loop(0, nt)
        def _(c):
            x_copy(c, d).wait_send()

    @pl.loop(1, nd)
    def _(d):
        d_copy(d).wait_send()
        r_copy(d).wait_send()


def attend_kernel(lengths, queries, cache, out):
    step = pl.program_id(0)
    length = lengths[step]
    cache_len = cache.shape[1]
    keys = cache[0, :, 0, :]
    values = cache[0, :, 1, :]
    group = QUERY_HEADS // KVH
    in_range = lax.broadcasted_iota(jnp.int32, (group, cache_len), 1) < length
    for k in range(KVH):
        at = slice(k * HEAD_SIZE, (k + 1) * HEAD_SIZE)
        q = queries[0, k * group:(k + 1) * group, :]
        scores = dot(q, keys[:, at], ((1,), (1,))) * (1.0 / math.sqrt(HEAD_SIZE))
        scores = jnp.where(in_range, scores, -jnp.inf)
        powers = jnp.exp(scores - jnp.max(scores, axis=1, keepdims=True))
        weights = (powers / jnp.sum(powers, axis=1, keepdims=True)).astype(BF16)
        out[0, k * group:(k + 1) * group, :] = dot(weights, values[:, at]).astype(BF16)


def attend(queries, key_value_cache, cached_lengths):
    own, cache_len, _, kv_width = key_value_cache.shape
    return pl.pallas_call(
        attend_kernel,
        out_shape=jax.ShapeDtypeStruct((own, QUERY_HEADS, HEAD_SIZE), BF16),
        grid_spec=pltpu.PrefetchScalarGridSpec(
            num_scalar_prefetch=1,
            grid=(own,),
            in_specs=[
                pl.BlockSpec((1, QUERY_HEADS, HEAD_SIZE), lambda i, n: (i, 0, 0)),
                pl.BlockSpec((1, cache_len, 2, kv_width), lambda i, n: (i, 0, 0, 0)),
            ],
            out_specs=pl.BlockSpec((1, QUERY_HEADS, HEAD_SIZE), lambda i, n: (i, 0, 0)),
        ),
    )(cached_lengths, queries, key_value_cache)


def local(hidden, query_weight, adapter_shrink, adapter_expand, adapter_page_table,
          request_adapter_index, key_value_cache, cached_lengths):
    nt, nd = lax.axis_size("tensor"), lax.axis_size("dp")
    own, width = hidden.shape
    rows = own * nt
    span = width // nt
    holders, _, rank = adapter_shrink.shape
    cols = query_weight.shape[1]
    slots = -(-3 * rows // (2 * nd) // 16) * 16
    matches = request_adapter_index[:, None] == jnp.arange(adapter_page_table.shape[0], dtype=jnp.int32)[None, :]
    pages = jnp.sum(jnp.where(matches, adapter_page_table[None, :], 0), axis=1)
    pages = jnp.broadcast_to(pages[:, None], (own, 128))
    vmem = pl.BlockSpec(memory_space=pltpu.VMEM)
    hbm = pl.BlockSpec(memory_space=pl.ANY)
    dma = pltpu.SemaphoreType.DMA
    queries = pl.pallas_call(
        query_kernel,
        out_shape=jax.ShapeDtypeStruct((nt, own, cols), BF16),
        in_specs=[vmem, vmem, hbm, hbm, hbm],
        out_specs=vmem,
        scratch_shapes=[
            pltpu.VMEM((nt, rows, span), BF16),
            pltpu.VMEM((rows, 128), jnp.int32),
            pltpu.VMEM((nt, span, cols), BF16),
            pltpu.VMEM(adapter_shrink.shape, BF16),
            pltpu.VMEM((holders * rank, cols), BF16),
            pltpu.VMEM((nd * slots, span + 128), BF16),
            pltpu.VMEM((nd * slots, span + 128), BF16),
            pltpu.VMEM((nd * slots, 128), F32),
            pltpu.VMEM((nt, nd * slots, 128), F32),
            pltpu.VMEM((nd * slots, cols), F32),
            pltpu.VMEM((nd * slots, cols), F32),
            pltpu.VMEM((rows, cols), BF16),
            pltpu.VMEM((rows, cols), F32),
            dma((nt,)), dma, dma, dma((nt,)), dma((nt,)), dma((nt,)), dma((nt, nt)), dma((nt, nt)),
            dma((nd,)), dma((nd,)), dma((nt,)), dma((nt,)), dma((nd,)), dma((nd,)), dma((nt,)), dma((nt,)),
        ],
        compiler_params=pltpu.CompilerParams(
            collective_id=0, has_side_effects=True, vmem_limit_bytes=56 * 1024 * 1024),
    )(hidden, pages, query_weight, adapter_shrink, adapter_expand.reshape(holders * rank, cols))
    queries = queries.transpose(1, 0, 2).reshape(own, QUERY_HEADS, HEAD_SIZE)
    attended = attend(queries, key_value_cache, cached_lengths)
    return attended.reshape(own, QUERY_HEADS * HEAD_SIZE)


def solution(mesh):
    in_specs = (
        P(("groups", "dp", "tensor"), None),
        P(None, "tensor"),
        P("dp", "tensor", None),
        P("dp", None, "tensor"),
        P("groups"),
        P(("groups", "dp", "tensor")),
        P(("groups", "dp", "tensor"), None, None, None),
        P(("groups", "dp", "tensor")),
    )
    out_specs = P(("groups", "dp", "tensor"), None)
    return jax.shard_map(local, mesh=mesh, in_specs=in_specs, out_specs=out_specs, check_vma=False)
```

time: 145 us -> 86.4 us (0.60)
  Pallas kernels: 0 us -> 72.8 us
  local copies, waits for them, and re-layouts: 40.6 us -> 12.4 us
  blocking collectives: 27.4 us -> 0 us
  waiting for transfers between devices: 26.9 us -> 0 us
  matrix products: 19.2 us -> 0 us
  between operations: 14.2 us -> 0.01 us
  starting transfers between devices: 13.5 us -> 0 us
    pallas_call x0 -> x2, Pallas kernels: none -> 72.8 us  [the longest x1 46.9 us: local(): pl.pallas_call(query_kernel, out_shape=jax.ShapeDtypeStruct((nt, own, col...]
    psum x1 -> x0, blocking collectives: 17.5 us -> none  [local(): lax.psum(partial_total_sum, 'tensor').astype(jnp.bfloat16)]
    dot_general x4 -> x0, matrix products: 15.8 us -> none  [the longest x1 9.46 us: local(): base_q = jnp.dot(row_x, query_weight, preferred_element_type=jnp.float32)]
    unnamed x13 -> x2, local copies, waits for them, and re-layouts: 24 us -> 9.98 us
    all_to_all x4 -> x0, waiting for transfers between devices: 13.7 us -> none  [the longest x1 7.29 us: local(): lax.all_to_all(send_x, 'dp', split_axis=0, concat_axis=0, tiled=True)]
    all_to_all x4 -> x0, starting transfers between devices: 13.5 us -> none  [the longest x1 3.46 us: local(): lax.all_to_all(send_x, 'dp', split_axis=0, concat_axis=0, tiled=True)]
    all_gather x1 -> x0, waiting for transfers between devices: 12.5 us -> none  [local(): lax.all_gather(hidden, 'tensor', axis=0, tiled=True)]
    slice x1 -> x0, local copies, waits for them, and re-layouts: 9.93 us -> none  [attend(): key_value_cache[:, :, 0, :].reshape(req_count, cache_len, KVH, HEAD_SIZE)]
  transfers between devices with their start and end apart: 5 -> 0, of which waited for: 3 -> 0; matrix products, arithmetic and copies ran while one was open for 27% -> 0% of each run, Pallas kernels for 0% -> 0%
where the time goes in v1:
time: 86.4 us; the launch traced here: 86 us
  Pallas kernels  72.8 us (84%)
  local copies, waits for them, and re-layouts  12.4 us (14%)
    pallas_call x1, Pallas kernels, local(): pl.pallas_call(query_kernel, out_shape=jax.ShapeDtypeStruct((nt, own, col...  46.9 us
    pallas_call x1, Pallas kernels, attend(): pl.pallas_call(attend_kernel, out_shape=jax.ShapeDtypeStruct((own, QUERY_...  25.9 us
    unnamed x2, local copies, waits for them, and re-layouts  9.98 us

profile of v1, /device:TPU:0, one launch (start us, length us, event | category | flops | bytes accessed | tf_op | source)
XLA Modules:
  0.0 86.0 jit_solution(4235864905686474324)
XLA Ops:
  0.0 0.9 select_reduce_fusion
  0.9 0.7 broadcast_in_dim.23.pages
  1.5 8.4 %copy.11.shrink = bf16[16,2048,64]{2,1,0:T(8,128)(2,1)} copy(bf16[16,2048,64]{1,2,0:T(8,128)(2,1)} %param.10) | data formatting | bytes 8388608 | tf_op args[2]
  9.9 46.9 %shard_map.82 = bf16[4,16,1024]{2,1,0:T(8,128)(2,1)} custom-call(bf16[16,8192]{1,0:T(8,128)(2,1)} %hidden.1, s32[16,128]{1,0:T(8,128)} %broadcast_in_dim.23.pages, bf16[8192,1024]{1,0:T(8,128)(2,1)} %weight.1, bf16[16,2048,64]{2,1,0:T(8,128)(2,1)} %copy.11.shrink, bf16[1024,1024]{1,0:T(8,128)(2,1)} %bitcast.6), custom_call_target="tpu_custom_call" | custom-call | tf_op jit(solution)/shard_map/pallas_call | solution.py:311
  56.8 1.0 %copy.12 = bf16[16,4,1024]{2,1,0:T(4,128)(2,1)S(1)} copy(bf16[16,4,1024]{2,0,1:T(8,128)(2,1)} %bitcast.7) | data formatting | bytes 262144 | tf_op jit(solution)/shard_map/transpose | solution.py:336
  57.8 0.7 reshape.13.queries
  58.5 25.9 %shard_map.83 = bf16[16,32,128]{2,1,0:T(8,128)(2,1)} custom-call(s32[16]{0:T(128)} %lengths.1, bf16[16,32,128]{2,1,0:T(8,128)(2,1)} %reshape.13.queries, bf16[16,128,2,512]{3,2,1,0:T(2,128)(2,1)} %cache.1), custom_call_target="tpu_custom_call" | custom-call | tf_op jit(solution)/shard_map/pallas_call | solution.py:281
  84.4 1.6 %copy.15 = bf16[2,8,32,128]{3,1,2,0:T(8,128)(2,1)} copy(bf16[2,8,32,128]{3,2,1,0:T(8,128)(2,1)} %bitcast.8) | data formatting | bytes 262144

commit v2 on v1

--- a/solution.py
+++ b/solution.py
@@ -11,6 +11,7 @@
 QUERY_HEADS = 32
 KVH = 4
 HEAD_SIZE = 128
+ADAPTER_RANK = 64
 MESH = pl.DeviceIdType.MESH
 F32 = jnp.float32
 BF16 = jnp.bfloat16
@@ -21,8 +22,9 @@
 
 
 def query_kernel(
-    hidden, pages, weight, shrink, expand,
+    lengths, hidden, pages, weight, shrink, expand, cache,
     out,
+    kv_in, kv, q_own, q_in, kv_sem,
     xg, pg, wv, sv, ev, xsend, xrecv, part, parts, ret_send, ret_recv, qsend, base,
     w_sem, s_sem, e_sem, own_sem, pg_send, pg_recv, x_send, x_recv,
     d_send, d_recv, p_send, p_recv, r_send, r_recv, q_send, q_recv,
@@ -32,7 +34,8 @@
     own, width = hidden.shape
     rows = own * nt
     span = width // nt
-    holders, rank = shrink.shape[0], shrink.shape[2]
+    rank = ADAPTER_RANK
+    holders = shrink.shape[0] // rank
     cols = weight.shape[1]
     slots = xsend.shape[0] // nd
     cap = 3 * rows // (2 * nd)
@@ -53,8 +56,10 @@
 
     s_copy = pltpu.make_async_copy(shrink, sv, s_sem)
     e_copy = pltpu.make_async_copy(expand, ev, e_sem)
+    kv_copy = pltpu.make_async_copy(cache, kv_in, kv_sem)
     w_copy(0).start()
     s_copy.start()
+    kv_copy.start()
     for c in range(1, nt):
         w_copy(c).start()
     e_copy.start()
@@ -148,6 +153,12 @@
 
     xrecv[my_slots, :] = xsend[my_slots, :]
 
+    kv_copy.wait()
+
+    def merge(i):
+        kv[i] = kv_in[i].reshape(kv.shape[1], kv.shape[2])
+
+    pl.loop(0, own // 2)(merge)
     w_copy(0).wait()
     tile = min(cols, 256)
 
@@ -166,12 +177,12 @@
         d_copy(d).wait_recv()
 
     resident = (xrecv[:, span:span + 128].astype(F32)).astype(jnp.int32)[:, 0:1] - 1 - g * holders
-    part[...] = jnp.zeros_like(part)
-
-    @pl.loop(0, holders)
-    def _(o):
-        y = dot(xrecv[:, :span], sv[o])
-        part[:, :rank] = part[:, :rank] + jnp.where(resident == o, y, 0.0)
+    shrunk = dot(xrecv[:, :span], sv[...], ((1,), (1,)))
+    half = lax.broadcasted_iota(jnp.int32, (nd * slots, 2 * rank), 1) // rank
+    acc = jnp.zeros((nd * slots, 2 * rank), F32)
+    for o in range(0, holders, 2):
+        acc = acc + jnp.where(resident == half + o, shrunk[:, o * rank:(o + 2) * rank], 0.0)
+    part[...] = acc
 
     def p_copy(d):
         return pltpu.make_async_remote_copy(
@@ -183,6 +194,7 @@
         p_copy(d).start()
 
     parts[t] = part[...]
+    pl.loop(own // 2, own)(merge)
 
     @pl.loop(1, nt)
     def _(c):
@@ -199,7 +211,7 @@
     total = parts[0]
     for i in range(1, nt):
         total = total + parts[i]
-    reduced = total[:, :rank].astype(BF16).astype(F32)
+    reduced = (total[:, :rank] + total[:, rank:]).astype(BF16).astype(F32)
     spread = jnp.concatenate(
         [jnp.where(resident == o, reduced, 0.0) for o in range(holders)], axis=1).astype(BF16)
     ret_send[...] = dot(spread, ev[...])
@@ -228,7 +240,7 @@
     def q_copy(d):
         p = tpeer(d)
         return pltpu.make_async_remote_copy(
-            src_ref=qsend.at[pl.ds(mult(p, own), own), :], dst_ref=out.at[t],
+            src_ref=qsend.at[pl.ds(mult(p, own), own), :], dst_ref=q_in.at[t],
             send_sem=q_send.at[d], recv_sem=q_recv.at[d],
             device_id={"tensor": p}, device_id_type=MESH)
 
@@ -236,11 +248,38 @@
     def _(d):
         q_copy(d).start()
 
-    out[t] = qsend[my_rows, :]
+    q_in[t] = qsend[my_rows, :]
 
     @pl.loop(1, nt)
     def _(d):
         q_copy(d).wait_recv()
+
+    heads = cols // HEAD_SIZE
+    for i in range(nt):
+        q_own[:, i * heads:(i + 1) * heads, :] = q_in[i].astype(F32).reshape(own, heads, HEAD_SIZE)
+
+    group = QUERY_HEADS // KVH
+    places, kv_width = kv.shape[1], kv.shape[2]
+    same = (lax.broadcasted_iota(jnp.int32, (QUERY_HEADS, kv_width), 0) // group
+            == lax.broadcasted_iota(jnp.int32, (QUERY_HEADS, kv_width), 1) // HEAD_SIZE)
+    spot = lax.broadcasted_iota(jnp.int32, (QUERY_HEADS, places), 1)
+    batch = 4
+
+    @pl.loop(0, own // batch)
+    def _(b):
+        for j in range(batch):
+            i = b * batch + j
+            q = jnp.where(same, jnp.concatenate([q_own[i]] * KVH, axis=1), 0.0).astype(BF16)
+            both = kv[i]
+            scores = dot(q, both, ((1,), (1,))) * (1.0 / math.sqrt(HEAD_SIZE))
+            scores = jnp.where((spot < 2 * lengths[i]) & (spot % 2 == 0), scores, -jnp.inf)
+            powers = jnp.exp(scores - jnp.max(scores, axis=1, keepdims=True))
+            weights = powers / jnp.sum(powers, axis=1, keepdims=True)
+            mixed = jnp.where(same, dot(pltpu.roll(weights, 1, 1).astype(BF16), both), 0.0)
+            mine = mixed[:, :HEAD_SIZE]
+            for k in range(1, KVH):
+                mine = mine + mixed[:, k * HEAD_SIZE:(k + 1) * HEAD_SIZE]
+            out[i] = mine.astype(BF16)
 
     @pl.loop(1, nt)
     def _(d):
@@ -256,41 +295,6 @@
     def _(d):
         d_copy(d).wait_send()
         r_copy(d).wait_send()
-
-
-def attend_kernel(lengths, queries, cache, out):
-    step = pl.program_id(0)
-    length = lengths[step]
-    cache_len = cache.shape[1]
-    keys = cache[0, :, 0, :]
-    values = cache[0, :, 1, :]
-    group = QUERY_HEADS // KVH
-    in_range = lax.broadcasted_iota(jnp.int32, (group, cache_len), 1) < length
-    for k in range(KVH):
-        at = slice(k * HEAD_SIZE, (k + 1) * HEAD_SIZE)
-        q = queries[0, k * group:(k + 1) * group, :]
-        scores = dot(q, keys[:, at], ((1,), (1,))) * (1.0 / math.sqrt(HEAD_SIZE))
-        scores = jnp.where(in_range, scores, -jnp.inf)
-        powers = jnp.exp(scores - jnp.max(scores, axis=1, keepdims=True))
-        weights = (powers / jnp.sum(powers, axis=1, keepdims=True)).astype(BF16)
-        out[0, k * group:(k + 1) * group, :] = dot(weights, values[:, at]).astype(BF16)
-
-
-def attend(queries, key_value_cache, cached_lengths):
-    own, cache_len, _, kv_width = key_value_cache.shape
-    return pl.pallas_call(
-        attend_kernel,
-        out_shape=jax.ShapeDtypeStruct((own, QUERY_HEADS, HEAD_SIZE), BF16),
-        grid_spec=pltpu.PrefetchScalarGridSpec(
-            num_scalar_prefetch=1,
-            grid=(own,),
-            in_specs=[
-                pl.BlockSpec((1, QUERY_HEADS, HEAD_SIZE), lambda i, n: (i, 0, 0)),
-                pl.BlockSpec((1, cache_len, 2, kv_width), lambda i, n: (i, 0, 0, 0)),
-            ],
-            out_specs=pl.BlockSpec((1, QUERY_HEADS, HEAD_SIZE), lambda i, n: (i, 0, 0)),
-        ),
-    )(cached_lengths, queries, key_value_cache)
 
 
 def local(hidden, query_weight, adapter_shrink, adapter_expand, adapter_page_table,
@@ -308,16 +312,22 @@
     vmem = pl.BlockSpec(memory_space=pltpu.VMEM)
     hbm = pl.BlockSpec(memory_space=pl.ANY)
     dma = pltpu.SemaphoreType.DMA
-    queries = pl.pallas_call(
+    cache_len, kv_width = key_value_cache.shape[1], key_value_cache.shape[3]
+    attended = pl.pallas_call(
         query_kernel,
-        out_shape=jax.ShapeDtypeStruct((nt, own, cols), BF16),
-        in_specs=[vmem, vmem, hbm, hbm, hbm],
+        out_shape=jax.ShapeDtypeStruct((own, QUERY_HEADS, HEAD_SIZE), BF16),
+        in_specs=[pl.BlockSpec(memory_space=pltpu.SMEM), vmem, vmem, hbm, hbm, hbm, hbm],
         out_specs=vmem,
         scratch_shapes=[
+            pltpu.VMEM(key_value_cache.shape, BF16),
+            pltpu.VMEM((own, 2 * cache_len, kv_width), BF16),
+            pltpu.VMEM((own, QUERY_HEADS, HEAD_SIZE), F32),
+            pltpu.VMEM((nt, own, cols), BF16),
+            dma,
             pltpu.VMEM((nt, rows, span), BF16),
             pltpu.VMEM((rows, 128), jnp.int32),
             pltpu.VMEM((nt, span, cols), BF16),
-            pltpu.VMEM(adapter_shrink.shape, BF16),
+            pltpu.VMEM((holders * rank, span), BF16),
             pltpu.VMEM((holders * rank, cols), BF16),
             pltpu.VMEM((nd * slots, span + 128), BF16),
             pltpu.VMEM((nd * slots, span + 128), BF16),
@@ -332,9 +342,9 @@
         ],
         compiler_params=pltpu.CompilerParams(
             collective_id=0, has_side_effects=True, vmem_limit_bytes=56 * 1024 * 1024),
-    )(hidden, pages, query_weight, adapter_shrink, adapter_expand.reshape(holders * rank, cols))
-    queries = queries.transpose(1, 0, 2).reshape(own, QUERY_HEADS, HEAD_SIZE)
-    attended = attend(queries, key_value_cache, cached_lengths)
+    )(cached_lengths, hidden, pages, query_weight,
+      jnp.swapaxes(adapter_shrink, 1, 2).reshape(holders * rank, span),
+      adapter_expand.reshape(holders * rank, cols), key_value_cache)
     return attended.reshape(own, QUERY_HEADS * HEAD_SIZE)
 
 

time: 86.4 us -> 59.2 us (0.69)
  Pallas kernels: 72.8 us -> 55.9 us
  local copies, waits for them, and re-layouts: 12.4 us -> 2.29 us
    pallas_call x2 -> x1, Pallas kernels: 72.8 us -> 55.9 us  [local(): pl.pallas_call(query_kernel, out_shape=jax.ShapeDtypeStruct((own, QUERY_H...]
    unnamed x2 -> x1, local copies, waits for them, and re-layouts: 9.98 us -> 1.61 us
    transpose x1 -> x0, local copies, waits for them, and re-layouts: 1.01 us -> none  [local(): queries = queries.transpose(1, 0, 2).reshape(own, QUERY_HEADS, HEAD_SIZE)]
where the time goes in v2:
time: 59.2 us; the launch traced here: 59.1 us
  Pallas kernels  55.9 us (94%)
  local copies, waits for them, and re-layouts  2.29 us (4%)
  other arithmetic  0.85 us (1%)
    pallas_call x1, Pallas kernels, local(): pl.pallas_call(query_kernel, out_shape=jax.ShapeDtypeStruct((own, QUERY_H...  55.9 us
    unnamed x1, local copies, waits for them, and re-layouts  1.61 us

profile of v2, /device:TPU:0, one launch (start us, length us, event | category | flops | bytes accessed | tf_op | source)
XLA Modules:
  0.0 59.1 jit_solution(10334928211874892091)
XLA Ops:
  0.0 0.9 %select_reduce_fusion = s32[16]{0:T(128)S(1)} fusion(s32[64]{0:T(128)} %param.12, s32[16]{0:T(128)} %param.13), kind=kLoop, calls=%fused_computation.1 | loop fusion | flops 3056 | bytes 384 | tf_op jit(solution)/shard_map/reduce_sum | solution.py:310
  0.9 0.7 %broadcast_in_dim.23.pages = s32[16,128]{1,0:T(8,128)} broadcast(s32[16]{0:T(128)S(1)} %select_reduce_fusion), dimensions={0} | broadcast | bytes 8256 | tf_op jit(solution)/shard_map/broadcast_in_dim | solution.py:311
  1.5 55.9 %shard_map.82 = bf16[16,32,128]{2,1,0:T(8,128)(2,1)} custom-call(s32[16]{0:T(128)} %lengths.1, bf16[16,8192]{1,0:T(8,128)(2,1)} %hidden.1, s32[16,128]{1,0:T(8,128)} %broadcast_in_dim.23.pages, bf16[8192,1024]{1,0:T(8,128)(2,1)} %weight.1, bf16[1024,2048]{1,0:T(8,128)(2,1)} %bitcast.8, bf16[1024,1024]{1,0:T(8,128)(2,1)} %bitcast.9, ...), custom_call_target="tpu_custom_call" | custom-call | tf_op jit(solution)/shard_map/pallas_call | solution.py:316
  57.5 1.6 %copy.11 = bf16[2,8,32,128]{3,1,2,0:T(8,128)(2,1)} copy(bf16[2,8,32,128]{3,2,1,0:T(8,128)(2,1)} %bitcast.10) | data formatting | bytes 262144
